TPU v7x, 32 devices: a whole 2x2x4 slice. The times are simulated.
32 devices in a mesh: grp: 2 (over y), gx: 16 (over z, x, core).
Axes of the slice: x: 2, y: 2, z: 4, core: 2. Of those that a mesh axis runs over, the one named last changes fastest.
Arguments:
- features: bfloat16 [128, 32, 64, 128], P('grp', 'gx'), parts along dimension 0, may hold values from -6 to 6
- cotangent: bfloat16 [128, 32, 64, 128], P('grp', 'gx'), parts along dimension 0, may hold values from -6 to 6
- spectral_weight: bfloat16 [16384, 64, 128], P('gx'), may hold values from -0.5 to 0.5
- channel_weight: bfloat16 [64, 64], replicated, may hold values from -0.75 to 0.75
- channel_bias: float32 [64], replicated, may hold values from -3 to 3
Outputs:
- activated: bfloat16 [128, 32, 64, 128], P('grp', 'gx'), parts along dimension 0
- feature_grad: bfloat16 [128, 32, 64, 128], P('grp', 'gx'), parts along dimension 0
- spectral_grad: bfloat16 [32768, 64, 128], P(('grp', 'gx')), parts along dimension 0
There are 2 independent parts, one for each index of `grp`. A program takes and returns all parts, laid end to end along the dimension named above; an argument that names none is the same for every part. Nothing has to cross between parts.
All inputs are finite; a program needn't handle non-finite values.
Results may differ from a plain program's by a relative error of at most 0.018.
Values may be sent and summed in bfloat16 or wider, within the bound.
A program may use at most 192 MiB of HBM per device.

v0:
```python
import math
import jax
import jax.numpy as jnp
from jax import lax
from jax.sharding import PartitionSpec as P

MX = 32
MY = 32
MZ = 16
SQRT_TWO_PI = math.sqrt(2.0 / math.pi)
CUBIC_COEF = 0.044715


def freq_index(retained, length):
    ladder = jnp.arange(retained, dtype=jnp.int32)
    return jnp.where(ladder < retained // 2, ladder, length - retained + ladder)


def cos_sin(wavenum, length):
    points = jnp.arange(length, dtype=jnp.int32)
    angles = (wavenum[:, None] * points[None, :] % length).astype(jnp.float32) * (
        2.0 * math.pi / length
    )
    return (jnp.cos(angles), jnp.sin(angles))


def analysis_pair(wavenum, length):
    cosine, sine_wave = cos_sin(wavenum, length)
    cosine, sine_wave = (cosine.T, sine_wave.T)
    return jnp.stack(
        [jnp.stack([cosine, -sine_wave], 1), jnp.stack([sine_wave, cosine], 1)], 1
    ).astype(jnp.bfloat16)


def synthesis_pair(wavenum, length):
    cosine, sine_wave = cos_sin(wavenum, length)
    return jnp.stack(
        [jnp.stack([cosine, sine_wave], 1), jnp.stack([-sine_wave, cosine], 1)], 1
    ).astype(jnp.bfloat16)


def depth_table(retained, length):
    cosine, sine_wave = cos_sin(jnp.arange(retained, dtype=jnp.int32), length)
    return jnp.concatenate([cosine, -sine_wave], 0).astype(jnp.bfloat16)


def gelu_parts(inputs):
    cubed_in = inputs * inputs * inputs
    tangent = jnp.tanh(SQRT_TWO_PI * (inputs + CUBIC_COEF * cubed_in))
    output = 0.5 * inputs * (1.0 + tangent)
    derivative = 0.5 * (1.0 + tangent) + 0.5 * inputs * (1.0 - tangent * tangent) * SQRT_TWO_PI * (
        1.0 + 3.0 * CUBIC_COEF * inputs * inputs
    )
    return (output, derivative)


def mode_product(coeffs, weights, channels):
    stacked = coeffs.reshape(coeffs.shape[0], 2, channels)
    halves = jnp.einsum("mac,mcj->amj", stacked, weights, preferred_element_type=jnp.float32)
    real_out = halves[0, :, :channels] - halves[1, :, channels:]
    imag_out = halves[0, :, channels:] + halves[1, :, :channels]
    return jnp.concatenate([real_out, imag_out], 1).astype(jnp.bfloat16)


def mode_grads(coeffs, weights, grad_modes, channels, weight_scale, input_scale):
    number = coeffs.shape[0]
    stacked = coeffs.reshape(number, 2, channels)
    grad_pairs = grad_modes.reshape(number, 2, channels)
    real_w = jnp.einsum("mac,mao->mco", stacked, grad_pairs, preferred_element_type=jnp.float32)
    imag_w = jnp.einsum(
        "mc,mo->mco", stacked[:, 0], grad_pairs[:, 1], preferred_element_type=jnp.float32
    ) - jnp.einsum(
        "mc,mo->mco", stacked[:, 1], grad_pairs[:, 0], preferred_element_type=jnp.float32
    )
    weight_grad = (jnp.concatenate([real_w, imag_w], 2) * weight_scale).astype(jnp.bfloat16)
    straight = jnp.concatenate([grad_pairs[:, 0], grad_pairs[:, 1]], 1)
    rotated = jnp.concatenate([grad_pairs[:, 1], -grad_pairs[:, 0]], 1)
    real_x = jnp.einsum("mcj,mj->mc", weights, straight, preferred_element_type=jnp.float32)
    imag_x = jnp.einsum("mcj,mj->mc", weights, rotated, preferred_element_type=jnp.float32)
    input_grad = (jnp.concatenate([real_x, imag_x], 1) * input_scale).astype(jnp.bfloat16)
    return (weight_grad, input_grad)


def body(features, cotangent, spectral_weight, channel_weight, channel_bias):
    channels, planes, lines, depth_len = features.shape
    devices = lax.axis_size("gx")
    all_planes = planes * devices
    first_plane = lax.axis_index("gx") * planes
    owned_modes = spectral_weight.shape[0]
    wave_pairs = MY * MZ
    forward_scale = 1.0 / math.sqrt(all_planes * lines * depth_len)
    inverse_scale = 1.0 / math.sqrt(MX * wave_pairs)
    weight_scale = math.sqrt(MX * wave_pairs / (all_planes * lines * depth_len))
    depth_basis = depth_table(MZ, depth_len)
    across_y = analysis_pair(freq_index(MY, lines), lines)
    back_y = synthesis_pair(freq_index(MY, lines), lines)
    across_full = analysis_pair(freq_index(MX, all_planes), all_planes)
    back_full = synthesis_pair(freq_index(MX, all_planes), all_planes)
    across_local = lax.dynamic_slice_in_dim(across_full, first_plane, planes, 0)
    back_local = lax.dynamic_slice_in_dim(back_full, first_plane, planes, 3)
    depth_part = jnp.dot(features, depth_basis.T, preferred_element_type=jnp.float32).astype(
        jnp.bfloat16
    )
    plane_part = (
        jnp.einsum(
            "cxyaz,yabk->cxbkz",
            depth_part.reshape(channels, planes, lines, 2, MZ),
            across_y,
            preferred_element_type=jnp.float32,
        )
        .astype(jnp.bfloat16)
        .reshape(channels, planes, 2, wave_pairs)
    )
    section = plane_part
    mode_sums = lax.psum_scatter(
        jnp.einsum(
            "cxaq,xabk->qkbc", section, across_local, preferred_element_type=jnp.float32
        ).reshape(lax.axis_size("gx") * owned_modes, 2 * channels),
        "gx",
        scatter_dimension=0,
        tiled=True,
    )
    coeffs = (mode_sums * forward_scale).astype(jnp.bfloat16)
    spectral = mode_product(coeffs, spectral_weight, channels)
    every_mode = lax.all_gather(spectral, "gx", axis=0, tiled=True)
    planes_back = jnp.einsum(
        "qkao,kabx->oxbq",
        every_mode.reshape(wave_pairs, MX, 2, channels),
        back_local,
        preferred_element_type=jnp.float32,
    ).astype(jnp.bfloat16)
    lines_back = (
        jnp.einsum(
            "oxakz,kaby->oxybz",
            planes_back.reshape(channels, planes, 2, MY, MZ),
            back_y,
            preferred_element_type=jnp.float32,
        )
        .astype(jnp.bfloat16)
        .reshape(channels, planes, lines, 2 * MZ)
    )
    spectral_term = (
        jnp.dot(lines_back, depth_basis, preferred_element_type=jnp.float32) * inverse_scale
    )
    pointwise = jnp.einsum(
        "oc,cxyz->oxyz", channel_weight, features, preferred_element_type=jnp.float32
    )
    hidden = spectral_term + pointwise + channel_bias[:, None, None, None]
    activated, derivative = gelu_parts(hidden)
    upstream = (cotangent.astype(jnp.float32) * derivative).astype(jnp.bfloat16)
    lines_grad = (
        jnp.dot(upstream, depth_basis.T, preferred_element_type=jnp.float32) * inverse_scale
    ).astype(jnp.bfloat16)
    rows_grad = (
        jnp.einsum(
            "oxybz,kaby->oxakz",
            lines_grad.reshape(channels, planes, lines, 2, MZ),
            back_y,
            preferred_element_type=jnp.float32,
        )
        .astype(jnp.bfloat16)
        .reshape(channels, planes, 2, wave_pairs)
    )
    section = rows_grad
    grad_sums = lax.psum_scatter(
        jnp.einsum(
            "oxbq,kabx->qkao", section, back_local, preferred_element_type=jnp.float32
        ).reshape(lax.axis_size("gx") * owned_modes, 2 * channels),
        "gx",
        scatter_dimension=0,
        tiled=True,
    )
    grad_modes = grad_sums.astype(jnp.bfloat16)
    spectral_grad, coeff_grad = mode_grads(
        coeffs, spectral_weight, grad_modes, channels, weight_scale, forward_scale
    )
    every_grad = lax.all_gather(coeff_grad, "gx", axis=0, tiled=True)
    plane_grad = jnp.einsum(
        "qkbc,xabk->cxaq",
        every_grad.reshape(wave_pairs, MX, 2, channels),
        across_local,
        preferred_element_type=jnp.float32,
    ).astype(jnp.bfloat16)
    depth_grad = (
        jnp.einsum(
            "cxbkz,yabk->cxyaz",
            plane_grad.reshape(channels, planes, 2, MY, MZ),
            across_y,
            preferred_element_type=jnp.float32,
        )
        .astype(jnp.bfloat16)
        .reshape(channels, planes, lines, 2 * MZ)
    )
    channel_back = jnp.einsum(
        "oc,oxyz->cxyz", channel_weight, upstream, preferred_element_type=jnp.float32
    )
    feature_grad = (
        jnp.dot(depth_grad, depth_basis, preferred_element_type=jnp.float32) + channel_back
    ).astype(jnp.bfloat16)
    return (activated.astype(jnp.bfloat16), feature_grad, spectral_grad)


def solution(mesh):
    in_specs = (
        P("grp", "gx", None, None),
        P("grp", "gx", None, None),
        P("gx", None, None),
        P(),
        P(),
    )
    out_specs = (
        P("grp", "gx", None, None),
        P("grp", "gx", None, None),
        P(("grp", "gx"), None, None),
    )
    return jax.shard_map(body, mesh=mesh, in_specs=in_specs, out_specs=out_specs, check_vma=False)
```

profile of v0, /device:TPU:0, one launch (start us, length us, event | category | flops | bytes accessed | tf_op | source)
XLA Modules:
  0.0 581.4 jit_solution(1618239725951916792)
XLA Ops:
  7.4 0.1 negate_convert_fusion.1
  7.5 0.2 negate_convert_fusion
  7.7 1.1 copy-done
  8.8 2.1 convolution_convert_fusion
  10.8 1.4 fusion.28
  12.2 0.2 copy.114
  12.4 0.3 copy.115
  12.7 4.8 convolution_bitcast_fusion.1
  17.5 16.1 %copy.116 = f32[512,32,2,64]{3,2,1,0:T(2,128)} copy(f32[512,32,2,64]{0,1,3,2:T(8,128)} %convolution_bitcast_fusion.1) | data formatting | bytes 16777216 | tf_op jit(solution)/shard_map/cxaq,xabk->qkbc/transpose | solution.py:116
  33.6 16.4 %reshape.402 = f32[16384,128]{1,0:T(8,128)} reshape(f32[512,32,2,64]{3,2,1,0:T(2,128)} %copy.116) | data formatting | bytes 16777216 | tf_op jit(solution)/shard_map/reshape | solution.py:118
  50.1 107.4 %reduce-scatter.3.cloned.1.call-done = f32[1024,128]{1,0:T(8,128)} async-done(((f32[16384,128]{1,0:T(8,128)}), f32[1024,128]{1,0:T(8,128)}) %reduce-scatter.3.cloned.1.call-update) | async-done | bytes 524304 | tf_op jit(solution)/shard_map/reduce_scatter | solution.py:115
  157.5 1.1 multiply_convert_fusion.2
  158.6 0.1 copy.117
  158.8 0.4 copy.118
  159.2 8.9 %fusion.114 = f32[1024,2,128]{2,1,0:T(2,128)} fusion(bf16[1024,2,64]{2,1,0:T(2,128)(2,1)S(1)} %copy.118, bf16[1024,64,128]{2,1,0:T(8,128)(2,1)} %param.7), kind=kOutput, calls=%fused_computation.163 | convolution fusion | flops 33554432 | bytes 18087936 | tf_op jit(solution)/shard_map/mac,mcj->amj/dot_general | solution.py:59
  168.0 2.3 copy.119
  170.3 1.2 fusion.57
  171.5 0.7 pad_maximum_fusion
  172.3 0.6 reduce-scatter.5.cloned.1.call-start
  172.9 0.2 fusion.103
  173.1 3.6 fusion.18
  176.7 46.1 %all-gather.3.cloned.1.call-done = bf16[16384,128]{0,1:T(8,128)(2,1)} async-done(((bf16[1024,128]{0,1:T(8,128)(2,1)}), bf16[16384,128]{0,1:T(8,128)(2,1)}) %all-gather.3.cloned.1.call-update) | async-done | bytes 4194320 | tf_op jit(solution)/shard_map/all_gather | solution.py:125
  222.8 6.4 %copy.120 = bf16[16384,128]{1,0:T(8,128)(2,1)} copy(bf16[16384,128]{0,1:T(8,128)(2,1)} %all-gather.3.cloned.1.call-done) | data formatting | bytes 8388608 | tf_op jit(solution)/shard_map/all_gather | solution.py:125
  229.2 14.7 %reshape.404 = bf16[512,32,2,64]{3,2,1,0:T(2,128)(2,1)} reshape(bf16[16384,128]{1,0:T(8,128)(2,1)} %copy.120) | data formatting | bytes 8388608 | tf_op jit(solution)/shard_map/reshape | solution.py:128
  243.9 15.3 %copy.122 = bf16[512,32,2,64]{0,1,2,3:T(8,128)(2,1)} copy(bf16[512,32,2,64]{3,2,1,0:T(2,128)(2,1)} %reshape.404) | data formatting | bytes 8388608 | tf_op jit(solution)/shard_map/reshape | solution.py:128
  259.2 3.0 fusion.41
  262.2 0.3 copy.123
  262.5 0.5 fusion.20
  263.0 2.5 copy.125
  265.4 11.8 %fusion.9 = (bf16[64,2,64,128]{3,2,1,0:T(8,128)(2,1)S(1)}, bf16[64,2,64,128]{3,2,1,0:T(8,128)(2,1)}) fusion(bf16[64,2,64,128]{3,2,1,0:T(8,128)(2,1)} %param.6, f32[64]{0:T(128)S(1)} %copy-done.9, f32[64,2,64,128]{3,0,2,1:T(8,128)} %fusion.18, bf16[64,2,64,32]{2,3,1,0:T(8,128)(2,1)} %bitcast.244, bf16[16,128]{1,0:T(8,128)(2,1)S(1)} %get-tuple-element.31, ...), kind=kOutput, calls=%fused_computation.13 | convolution fusion | flops 93339648 | bytes 11018496 | tf_op jit(solution)/shard_map/dot_general | solution.py:143
  277.2 2.1 multiply_convert_fusion.1
  279.3 1.4 fusion.27
  280.7 1.0 copy.130
  281.7 1.3 copy.132
  283.0 4.6 convolution_bitcast_fusion
  287.6 16.1 %copy.133 = f32[512,32,2,64]{3,2,1,0:T(2,128)} copy(f32[512,32,2,64]{0,1,3,2:T(8,128)} %convolution_bitcast_fusion) | data formatting | bytes 16777216 | tf_op jit(solution)/shard_map/oxbq,kabx->qkao/transpose | solution.py:166
  303.8 16.4 %reshape.409 = f32[16384,128]{1,0:T(8,128)} reshape(f32[512,32,2,64]{3,2,1,0:T(2,128)} %copy.133) | data formatting | bytes 16777216 | tf_op jit(solution)/shard_map/reshape | solution.py:168
  320.3 103.3 %reduce-scatter.5.cloned.1.call-done = f32[1024,128]{1,0:T(8,128)} async-done(((f32[16384,128]{1,0:T(8,128)}), f32[1024,128]{1,0:T(8,128)}) %reduce-scatter.5.cloned.1.call-update) | async-done | bytes 524304 | tf_op jit(solution)/shard_map/reduce_scatter | solution.py:165
  423.5 1.1 convert_element_type.187
  424.6 0.1 copy.134
  424.8 0.9 fusion.111
  425.7 0.8 maximum_bitcast_fusion
  426.4 2.1 copy.164
  428.6 13.0 %fusion.115 = f32[1024,1,64]{2,1,0:T(1,128)} fusion(bf16[1024,128,1]{1,2,0:T(2,128)(2,1)} %copy.164, bf16[1024,64,128]{2,1,0:T(8,128)(2,1)} %param.7), kind=kOutput, calls=%fused_computation.164 | convolution fusion | flops 16777216 | bytes 17301504 | tf_op jit(solution)/shard_map/mcj,mj->mc/dot_general | solution.py:78
  441.6 1.1 copy.166
  442.7 12.4 %fusion.116 = f32[1024,1,64]{2,1,0:T(1,128)S(1)} fusion(bf16[1024,128,1]{1,2,0:T(2,128)(2,1)} %copy.166, bf16[1024,64,128]{2,1,0:T(8,128)(2,1)} %param.7), kind=kOutput, calls=%fused_computation.165 | convolution fusion | flops 16777216 | bytes 17301504 | tf_op jit(solution)/shard_map/mcj,mj->mc/dot_general | solution.py:79
  455.1 0.9 fusion.48
  456.1 0.8 fusion.60
  456.9 1.1 copy.146
  458.0 2.0 copy.148
  460.0 3.7 fusion.16
  463.7 0.4 copy.145
  464.0 1.2 copy.147
  465.2 1.1 copy.149
  466.4 12.4 %fusion.117 = f32[1024,64,64]{2,1,0:T(8,128)} fusion(bf16[1024,2,64]{2,1,0:T(2,128)(2,1)S(1)} %copy.118, bf16[1024,2,64]{2,1,0:T(2,128)(2,1)S(1)} %copy.145), kind=kOutput, calls=%fused_computation.166 | convolution fusion | flops 16777216 | bytes 17301504 | tf_op jit(solution)/shard_map/mac,mao->mco/dot_general | solution.py:69
  478.8 22.8 %multiply_subtract_fusion = f32[1024,64,64]{2,1,0:T(8,128)} fusion(f32[1024,64]{1,0:T(8,128)S(1)} %copy.149, f32[1024,64]{1,0:T(8,128)S(1)} %copy-done.2, f32[1024,64]{1,0:T(8,128)S(1)} %copy.147, f32[1024,64]{1,0:T(8,128)S(1)} %copy.146), kind=kLoop, calls=%fused_computation.2 | loop fusion | flops 12582912 | bytes 17825792 | tf_op jit(solution)/shard_map/sub | solution.py:70
  501.7 28.5 %fusion = bf16[1024,64,128]{2,1,0:T(8,128)(2,1)} fusion(f32[1024,64,64]{2,1,0:T(8,128)} %multiply_subtract_fusion, f32[1024,64,64]{2,1,0:T(8,128)} %fusion.117), kind=kLoop, calls=%fused_computation.1 | loop fusion | flops 25165824 | bytes 50331648 | tf_op jit(solution)/shard_map/convert_element_type | solution.py:75
  530.1 14.8 %reshape.411 = bf16[512,32,2,64]{3,2,1,0:T(2,128)(2,1)} reshape(bf16[16384,128]{1,0:T(8,128)(2,1)} %all-gather.5.cloned.1.call-done) | data formatting | bytes 8388608 | tf_op jit(solution)/shard_map/reshape | solution.py:180
  544.9 15.5 %copy.136 = bf16[512,32,2,64]{0,1,2,3:T(8,128)(2,1)} copy(bf16[512,32,2,64]{3,2,1,0:T(2,128)(2,1)} %reshape.411) | data formatting | bytes 8388608 | tf_op jit(solution)/shard_map/reshape | solution.py:180
  560.4 2.9 fusion.38
  563.3 0.3 copy.137
  563.7 0.5 fusion.21
  564.1 2.3 copy.140
  566.5 7.9 %fusion.10 = bf16[64,2,64,128]{3,2,1,0:T(8,128)(2,1)} fusion(f32[2,64,128,64]{2,3,1,0:T(8,128)} %fusion.16, bf16[64,2,64,32]{2,3,1,0:T(8,128)(2,1)} %bitcast.234, bf16[16,128]{1,0:T(8,128)(2,1)S(1)} %get-tuple-element.31, bf16[16,128]{1,0:T(8,128)(2,1)S(1)} %get-tuple-element.32), kind=kOutput, calls=%fused_computation.15 | convolution fusion | flops 69222400 | bytes 6823936 | tf_op jit(solution)/shard_map/dot_general | solution.py:198
  (35 shorter events, 0.5 us)
Async XLA Ops:
  7.2 1.6 copy-start
  7.2 150.4 %reduce-scatter.3.cloned.1.call-start = ((), (), s32[]{:S(2)}) async-start(), calls=%async_computation.2 | async-start | bytes 8912896 | tf_op jit(solution)/shard_map/reduce_scatter | solution.py:115
  7.7 4.7 copy-start.4
  7.7 4.7 copy-start.6
  50.1 172.7 %all-gather.3.cloned.1.call-start = ((), (), s32[]{:S(2)}) async-start(), calls=%async_computation.3 | async-start | bytes 4456448 | tf_op jit(solution)/shard_map/all_gather | solution.py:125
  168.0 5.0 copy-start.8
  172.3 251.3 %reduce-scatter.5.cloned.1.call-start = ((), (), s32[]{:S(2)}) async-start(), calls=%async_computation.4 | async-start | bytes 8912896 | tf_op jit(solution)/shard_map/reduce_scatter | solution.py:165
  259.2 6.3 %copy-start.9 = (f32[64]{0:T(128)S(1)}, f32[64]{0:T(128)}, u32[]{:S(2)}) copy-start(f32[64]{0:T(128)} %param.9) | copy-start | bytes 772
  320.2 209.9 %all-gather.5.cloned.1.call-start = ((), (), s32[]{:S(2)}) async-start(), calls=%async_computation.5 | async-start | bytes 4456448 | tf_op jit(solution)/shard_map/all_gather | solution.py:177
  442.7 12.4 %copy-start.3 = (f32[1024,1,64]{2,1,0:T(1,128)S(1)}, f32[1024,1,64]{2,1,0:T(1,128)}, u32[]{:S(2)}) copy-start(f32[1024,1,64]{2,1,0:T(1,128)} %fusion.115) | copy-start | bytes 786436
  466.4 12.5 %copy-start.2 = (f32[1024,64]{1,0:T(8,128)S(1)}, f32[1024,64]{1,0:T(8,128)}, u32[]{:S(2)}) copy-start(f32[1024,64]{1,0:T(8,128)} %copy.148) | copy-start | bytes 786436
  560.4 3.3 copy-start.5
  560.4 3.3 copy-start.7
  564.1 10.3 %copy-start.1 = (bf16[64,2,64,128]{3,2,1,0:T(8,128)(2,1)S(1)}, bf16[64,2,64,128]{3,2,1,0:T(8,128)(2,1)}, u32[]{:S(2)}) copy-start(bf16[64,2,64,128]{3,2,1,0:T(8,128)(2,1)} %param.5) | copy-start | bytes 6291460
Sparse Core Ops, SparseCore 0:
  50.2 107.2 reduce-scatter.2
  172.4 50.3 all-gather.2
  320.3 103.1 reduce-scatter.4
  456.2 50.4 all-gather.4
where the time goes:
time: 591 us; the launch traced here: 581 us
  waiting for transfers between devices  257 us (43%)
  local copies, waits for them, and re-layouts  153 us (26%)
  matrix products  96.8 us (16%)
  other arithmetic  59.4 us (10%)
  between operations  14.5 us (2%)
    reduce_scatter x1, waiting for transfers between devices, body(): lax.psum_scatter(jnp.einsum('cxaq,xabk->qkbc', section, across_local, pre...  107 us
    reduce_scatter x1, waiting for transfers between devices, body(): lax.psum_scatter(jnp.einsum('oxbq,kabx->qkao', section, back_local, prefe...  103 us
    all_gather x1, waiting for transfers between devices, body(): every_mode = lax.all_gather(spectral, 'gx', axis=0, tiled=True)  46.1 us
    reshape x2, local copies, waits for them, and re-layouts, body(): every_grad.reshape(wave_pairs, MX, 2, channels)  30.3 us
    reshape x2, local copies, waits for them, and re-layouts, body(): every_mode.reshape(wave_pairs, MX, 2, channels)  30 us
    convert_element_type x1, other arithmetic, mode_grads(): (jnp.concatenate([real_w, imag_w], 2) * weight_scale).astype(jnp.bfloat16)  28.5 us
    sub x1, other arithmetic, mode_grads(): jnp.einsum('mc,mo->mco', stacked[:, 0], grad_pairs[:, 1], preferred_eleme...  22.8 us
    reshape x1, local copies, waits for them, and re-layouts, body(): mode_sums = lax.psum_scatter(jnp.einsum('cxaq,xabk->qkbc', section, acros...  16.4 us
  transfers between devices with their start and end apart: 4, of which 3 were waited for; matrix products, arithmetic and copies ran while one was open for 13% of the time, Pallas kernels for 0%

commit v1 on v0

--- a/solution.py
+++ b/solution.py
@@ -3,6 +3,7 @@
 import jax.numpy as jnp
 from jax import lax
 from jax.sharding import PartitionSpec as P
+from jax.lax import axis_index, axis_size, ppermute
 
 MX = 32
 MY = 32
@@ -122,7 +123,19 @@
     )
     coeffs = (mode_sums * forward_scale).astype(jnp.bfloat16)
     spectral = mode_product(coeffs, spectral_weight, channels)
-    every_mode = lax.all_gather(spectral, "gx", axis=0, tiled=True)
+    slots = axis_size("gx")
+    stack_in = [(s, (s + 1) % slots) for s in range(slots)]
+    queue = [(s, (s - 1) % slots) for s in range(slots)]
+    k_now, odd = ([spectral], [spectral])
+    for _ in range(slots // 2):
+        local_now = ppermute(k_now[-1], axis_name="gx", perm=stack_in)
+        k_now.append(local_now)
+    for _ in tuple(range((slots - 1) // 2)):
+        prior = ppermute(odd[-1], axis_name="gx", perm=queue)
+        odd.append(prior)
+    before = jnp.concatenate([*k_now[::-1], *odd[1:]], 0)
+    step_out = axis_index("gx")
+    every_mode = jnp.roll(before, (step_out - slots // 2) * spectral.shape[0], 0)
     planes_back = jnp.einsum(
         "qkao,kabx->oxbq",
         every_mode.reshape(wave_pairs, MX, 2, channels),

time: 591 us -> 638 us (1.080)
  starting transfers between devices: 0.69 us -> 45.4 us
  local copies, waits for them, and re-layouts: 153 us -> 165 us
  waiting for transfers between devices: 257 us -> 245 us
    all_gather x1 -> x0, waiting for transfers between devices: 46.1 us -> none  [body(): every_mode = lax.all_gather(spectral, 'gx', axis=0, tiled=True)]
    ppermute x0 -> x15, starting transfers between devices: none -> 45.3 us  [the longest x7 45.2 us: body(): prior = ppermute(odd[-1], axis_name='gx', perm=queue)]
    ppermute x0 -> x15, waiting for transfers between devices: none -> 31.7 us  [the longest x8 29 us: body(): local_now = ppermute(k_now[-1], axis_name='gx', perm=stack_in)]
    unnamed x20 -> x69, local copies, waits for them, and re-layouts: 1.14 us -> 10.1 us
    dynamic_slice x0 -> x2, local copies, waits for them, and re-layouts: none -> 8.74 us  [body(): jnp.roll(before, (step_out - slots // 2) * spectral.shape[0], 0)]
    all_gather x1 -> x0, local copies, waits for them, and re-layouts: 6.41 us -> none  [body(): every_mode = lax.all_gather(spectral, 'gx', axis=0, tiled=True)]
  transfers between devices with their start and end apart: 4 -> 18, of which waited for: 3 -> 13; matrix products, arithmetic and copies ran while one was open for 13% -> 13% of each run, Pallas kernels for 0% -> 0%
where the time goes in v1:
time: 638 us; the launch traced here: 626 us
  waiting for transfers between devices  245 us (38%)
  local copies, waits for them, and re-layouts  165 us (26%)
  matrix products  97.9 us (15%)
  other arithmetic  58.7 us (9%)
  starting transfers between devices  45.4 us (7%)
  between operations  14.6 us (2%)
    reduce_scatter x1, waiting for transfers between devices, body(): lax.psum_scatter(jnp.einsum('cxaq,xabk->qkbc', section, across_local, pre...  107 us
    reduce_scatter x1, waiting for transfers between devices, body(): lax.psum_scatter(jnp.einsum('oxbq,kabx->qkao', section, back_local, prefe...  106 us
    ppermute x7, starting transfers between devices, body(): prior = ppermute(odd[-1], axis_name='gx', perm=queue)  45.2 us
    reshape x2, local copies, waits for them, and re-layouts, body(): every_grad.reshape(wave_pairs, MX, 2, channels)  30.4 us
    reshape x2, local copies, waits for them, and re-layouts, body(): every_mode.reshape(wave_pairs, MX, 2, channels)  30 us
    ppermute x8, waiting for transfers between devices, body(): local_now = ppermute(k_now[-1], axis_name='gx', perm=stack_in)  29 us
    convert_element_type x1, other arithmetic, mode_grads(): (jnp.concatenate([real_w, imag_w], 2) * weight_scale).astype(jnp.bfloat16)  28.4 us
    sub x1, other arithmetic, mode_grads(): jnp.einsum('mc,mo->mco', stacked[:, 0], grad_pairs[:, 1], preferred_eleme...  22.8 us
  transfers between devices with their start and end apart: 18, of which 13 were waited for; matrix products, arithmetic and copies ran while one was open for 13% of the time, Pallas kernels for 0%

profile of v1, /device:TPU:0, one launch (start us, length us, event | category | flops | bytes accessed | tf_op | source)
XLA Modules:
  0.0 626.2 jit_solution(8137123711990404314)
XLA Ops:
  7.7 1.1 copy-done
  8.8 2.1 convolution_convert_fusion
  10.8 1.4 fusion.28
  12.7 4.8 convolution_bitcast_fusion.1
  17.5 16.1 %copy.115 = f32[512,32,2,64]{3,2,1,0:T(2,128)} copy(f32[512,32,2,64]{0,1,3,2:T(8,128)} %convolution_bitcast_fusion.1) | data formatting | bytes 16777216 | tf_op jit(solution)/shard_map/cxaq,xabk->qkbc/transpose | solution.py:117
  33.7 16.4 %reshape.402 = f32[16384,128]{1,0:T(8,128)} reshape(f32[512,32,2,64]{3,2,1,0:T(2,128)} %copy.115) | data formatting | bytes 16777216 | tf_op jit(solution)/shard_map/reshape | solution.py:119
  50.1 107.4 %reduce-scatter.3.cloned.1.call-done = f32[1024,128]{1,0:T(8,128)} async-done(((f32[16384,128]{1,0:T(8,128)}), f32[1024,128]{1,0:T(8,128)}) %reduce-scatter.3.cloned.1.call-update) | async-done | bytes 524304 | tf_op jit(solution)/shard_map/reduce_scatter | solution.py:116
  157.5 1.1 multiply_convert_fusion.2
  159.2 8.9 %fusion.114 = f32[1024,2,128]{2,1,0:T(2,128)} fusion(bf16[1024,2,64]{2,1,0:T(2,128)(2,1)S(1)} %copy.117, bf16[1024,64,128]{2,1,0:T(8,128)(2,1)} %param.7), kind=kOutput, calls=%fused_computation.196 | convolution fusion | flops 33554432 | bytes 18087936 | tf_op jit(solution)/shard_map/mac,mcj->amj/dot_general | solution.py:60
  168.0 2.2 copy.118
  170.3 1.2 fusion.57
  171.6 8.5 %collective-permute-done = bf16[1024,128]{0,1:T(8,128)(2,1)S(1)} collective-permute-done((bf16[1024,128]{0,1:T(8,128)(2,1)S(1)}, bf16[1024,128]{0,1:T(8,128)(2,1)S(1)}, u32[]{:S(2)}, u32[]{:S(2)}) %collective-permute-start) | collective-permute-done | bytes 262176 | tf_op jit(solution)/shard_map/ppermute | solution.py:131
  180.1 4.4 collective-permute-start.8
  184.5 4.1 collective-permute-done.1
  189.3 4.5 collective-permute-start.9
  193.8 3.3 collective-permute-done.2
  197.7 4.7 collective-permute-start.10
  202.5 3.3 collective-permute-done.3
  206.4 4.8 collective-permute-start.11
  211.2 3.3 collective-permute-done.4
  215.4 4.7 collective-permute-start.12
  220.1 3.3 collective-permute-done.5
  224.3 4.6 collective-permute-start.13
  228.9 3.2 collective-permute-done.6
  232.1 3.7 fusion.18
  235.8 17.4 %collective-permute-start.14 = (bf16[1024,128]{0,1:T(8,128)(2,1)S(1)}, bf16[1024,128]{0,1:T(8,128)(2,1)S(1)}, u32[]{:S(2)}, u32[]{:S(2)}) collective-permute-start(bf16[1024,128]{0,1:T(8,128)(2,1)S(1)} %collective-permute-done.13), channel_id=1, source_target_pairs={{0,15},{1,0},{2,1},{3,2},{4,3},{5,4},{6,5},{7,6},{8,7},{9,8},{10,9... | collective-permute-start | bytes 786440 | tf_op jit(solution)/shard_map/ppermute | solution.py:134
  253.3 1.0 constant_dynamic-update-slice_fusion.29
  254.2 1.0 constant_dynamic-update-slice_fusion.28
  259.7 1.0 constant_dynamic-update-slice_fusion.4
  261.7 2.3 constant_dynamic-slice_fusion
  264.0 6.4 %copy.119 = bf16[16384,128]{1,0:T(8,128)(2,1)} copy(bf16[16384,128]{0,1:T(8,128)(2,1)} %constant_dynamic-slice_fusion) | data formatting | bytes 8388608 | tf_op jit(solution)/shard_map/jit(_roll_dynamic)/dynamic_slice | solution.py:138
  270.4 14.7 %reshape.404 = bf16[512,32,2,64]{3,2,1,0:T(2,128)(2,1)} reshape(bf16[16384,128]{1,0:T(8,128)(2,1)} %copy.119) | data formatting | bytes 8388608 | tf_op jit(solution)/shard_map/reshape | solution.py:141
  285.1 15.3 %copy.121 = bf16[512,32,2,64]{0,1,2,3:T(8,128)(2,1)} copy(bf16[512,32,2,64]{3,2,1,0:T(2,128)(2,1)} %reshape.404) | data formatting | bytes 8388608 | tf_op jit(solution)/shard_map/reshape | solution.py:141
  300.4 3.0 fusion.41
  304.2 2.3 copy.124
  306.5 11.8 %fusion.9 = (bf16[64,2,64,128]{3,2,1,0:T(8,128)(2,1)S(1)}, bf16[64,2,64,128]{3,2,1,0:T(8,128)(2,1)}) fusion(bf16[64,2,64,128]{3,2,1,0:T(8,128)(2,1)} %param.6, f32[64]{0:T(128)S(1)} %copy-done.19, f32[64,2,64,128]{3,0,2,1:T(8,128)} %fusion.18, bf16[64,2,64,32]{2,3,1,0:T(8,128)(2,1)} %bitcast.244, bf16[16,128]{1,0:T(8,128)(2,1)S(1)} %get-tuple-element.31, ...), kind=kOutput, calls=%fused_computation.13 | convolution fusion | flops 93339648 | bytes 11018496 | tf_op jit(solution)/shard_map/dot_general | solution.py:156
  318.3 2.1 multiply_convert_fusion.1
  320.4 1.4 fusion.27
  321.8 1.0 copy.129
  322.8 1.3 copy.131
  324.1 4.7 convolution_bitcast_fusion
  328.7 16.1 %copy.132 = f32[512,32,2,64]{3,2,1,0:T(2,128)} copy(f32[512,32,2,64]{0,1,3,2:T(8,128)} %convolution_bitcast_fusion) | data formatting | bytes 16777216 | tf_op jit(solution)/shard_map/oxbq,kabx->qkao/transpose | solution.py:179
  344.9 16.4 %reshape.409 = f32[16384,128]{1,0:T(8,128)} reshape(f32[512,32,2,64]{3,2,1,0:T(2,128)} %copy.132) | data formatting | bytes 16777216 | tf_op jit(solution)/shard_map/reshape | solution.py:181
  361.3 105.6 %reduce-scatter.5.cloned.1.call-done = f32[1024,128]{1,0:T(8,128)} async-done(((f32[16384,128]{1,0:T(8,128)}), f32[1024,128]{1,0:T(8,128)}) %reduce-scatter.5.cloned.1.call-update) | async-done | bytes 524304 | tf_op jit(solution)/shard_map/reduce_scatter | solution.py:178
  466.9 1.1 convert_element_type.187
  469.8 2.0 copy.163
  471.8 13.0 %fusion.115 = f32[1024,1,64]{2,1,0:T(1,128)} fusion(bf16[1024,128,1]{1,2,0:T(2,128)(2,1)} %copy.163, bf16[1024,64,128]{2,1,0:T(8,128)(2,1)} %param.7), kind=kOutput, calls=%fused_computation.197 | convolution fusion | flops 16777216 | bytes 17301504 | tf_op jit(solution)/shard_map/mcj,mj->mc/dot_general | solution.py:79
  484.8 1.1 copy.165
  485.9 12.4 %fusion.116 = f32[1024,1,64]{2,1,0:T(1,128)S(1)} fusion(bf16[1024,128,1]{1,2,0:T(2,128)(2,1)} %copy.165, bf16[1024,64,128]{2,1,0:T(8,128)(2,1)} %param.7), kind=kOutput, calls=%fused_computation.198 | convolution fusion | flops 16777216 | bytes 17301504 | tf_op jit(solution)/shard_map/mcj,mj->mc/dot_general | solution.py:80
  500.1 1.1 copy.145
  501.2 2.0 copy.147
  503.2 3.7 fusion.16
  507.2 1.2 copy.146
  508.4 1.1 copy.148
  509.6 12.4 %fusion.117 = f32[1024,64,64]{2,1,0:T(8,128)} fusion(bf16[1024,2,64]{2,1,0:T(2,128)(2,1)S(1)} %copy.117, bf16[1024,2,64]{2,1,0:T(2,128)(2,1)S(1)} %copy.144), kind=kOutput, calls=%fused_computation.199 | convolution fusion | flops 16777216 | bytes 17301504 | tf_op jit(solution)/shard_map/mac,mao->mco/dot_general | solution.py:70
  522.0 22.8 %multiply_subtract_fusion = f32[1024,64,64]{2,1,0:T(8,128)} fusion(f32[1024,64]{1,0:T(8,128)S(1)} %copy.148, f32[1024,64]{1,0:T(8,128)S(1)} %copy-done.2, f32[1024,64]{1,0:T(8,128)S(1)} %copy.146, f32[1024,64]{1,0:T(8,128)S(1)} %copy.145), kind=kLoop, calls=%fused_computation.2 | loop fusion | flops 12582912 | bytes 17825792 | tf_op jit(solution)/shard_map/sub | solution.py:71
  544.8 28.4 %fusion = bf16[1024,64,128]{2,1,0:T(8,128)(2,1)} fusion(f32[1024,64,64]{2,1,0:T(8,128)} %multiply_subtract_fusion, f32[1024,64,64]{2,1,0:T(8,128)} %fusion.117), kind=kLoop, calls=%fused_computation.1 | loop fusion | flops 25165824 | bytes 50331648 | tf_op jit(solution)/shard_map/convert_element_type | solution.py:76
  573.3 14.7 %reshape.411 = bf16[512,32,2,64]{3,2,1,0:T(2,128)(2,1)} reshape(bf16[16384,128]{1,0:T(8,128)(2,1)} %all-gather.2.cloned.1.call-done) | data formatting | bytes 8388608 | tf_op jit(solution)/shard_map/reshape | solution.py:193
  588.0 15.6 %copy.135 = bf16[512,32,2,64]{0,1,2,3:T(8,128)(2,1)} copy(bf16[512,32,2,64]{3,2,1,0:T(2,128)(2,1)} %reshape.411) | data formatting | bytes 8388608 | tf_op jit(solution)/shard_map/reshape | solution.py:193
  603.7 2.9 fusion.38
  606.6 1.0 copy.136
  607.6 1.5 fusion.21
  609.1 2.4 copy.139
  611.5 7.9 %fusion.10 = bf16[64,2,64,128]{3,2,1,0:T(8,128)(2,1)} fusion(f32[2,64,128,64]{2,3,1,0:T(8,128)} %fusion.16, bf16[64,2,64,32]{2,3,1,0:T(8,128)(2,1)} %bitcast.234, bf16[16,128]{1,0:T(8,128)(2,1)S(1)} %get-tuple-element.31, bf16[16,128]{1,0:T(8,128)(2,1)S(1)} %get-tuple-element.32), kind=kOutput, calls=%fused_computation.15 | convolution fusion | flops 69222400 | bytes 6823936 | tf_op jit(solution)/shard_map/dot_general | solution.py:211
  (115 shorter events, 15.4 us)
Async XLA Ops:
  7.2 1.6 copy-start
  7.2 150.3 %reduce-scatter.3.cloned.1.call-start = ((), (), s32[]{:S(2)}) async-start(), calls=%async_computation.2 | async-start | bytes 8912896 | tf_op jit(solution)/shard_map/reduce_scatter | solution.py:116
  7.7 4.7 copy-start.14
  7.7 4.7 copy-start.16
  50.1 416.9 %reduce-scatter.5.cloned.1.call-start = ((), (), s32[]{:S(2)}) async-start(), calls=%async_computation.3 | async-start | bytes 8912896 | tf_op jit(solution)/shard_map/reduce_scatter | solution.py:178
  159.1 73.0 %copy-start.18 = (bf16[64,64]{1,0:T(8,128)(2,1)S(1)}, bf16[64,64]{1,0:T(8,128)(2,1)}, u32[]{:S(2)}) copy-start(bf16[64,64]{1,0:T(8,128)(2,1)} %param.8) | copy-start | bytes 24580
  171.5 8.5 %collective-permute-start = (bf16[1024,128]{0,1:T(8,128)(2,1)S(1)}, bf16[1024,128]{0,1:T(8,128)(2,1)S(1)}, u32[]{:S(2)}, u32[]{:S(2)}) collective-permute-start(bf16[1024,128]{0,1:T(8,128)(2,1)S(1)} %pad_maximum_fusion), channel_id=1, source_target_pairs={{0,1},{1,2},{2,3},{3,4},{4,5},{5,6},{6,7},{7,8},{8,9},{9,10},{10,1... | collective-permute-start | bytes 786440 | tf_op jit(solution)/shard_map/ppermute | solution.py:131
  180.1 8.5 %collective-permute-start.1 = (bf16[1024,128]{0,1:T(8,128)(2,1)S(1)}, bf16[1024,128]{0,1:T(8,128)(2,1)S(1)}, u32[]{:S(2)}, u32[]{:S(2)}) collective-permute-start(bf16[1024,128]{0,1:T(8,128)(2,1)S(1)} %collective-permute-done), channel_id=1, source_target_pairs={{0,1},{1,2},{2,3},{3,4},{4,5},{5,6},{6,7},{7,8},{8,9},{9,10},{10,1... | collective-permute-start | bytes 786440 | tf_op jit(solution)/shard_map/ppermute | solution.py:131
  180.1 8.5 %collective-permute-start.8 = (bf16[1024,128]{0,1:T(8,128)(2,1)S(1)}, bf16[1024,128]{0,1:T(8,128)(2,1)S(1)}, u32[]{:S(2)}, u32[]{:S(2)}) collective-permute-start(bf16[1024,128]{0,1:T(8,128)(2,1)S(1)} %pad_maximum_fusion), channel_id=1, source_target_pairs={{0,15},{1,0},{2,1},{3,2},{4,3},{5,4},{6,5},{7,6},{8,7},{9,8},{10,9... | collective-permute-start | bytes 786440 | tf_op jit(solution)/shard_map/ppermute | solution.py:134
  188.6 9.2 %copy-start.5 = (bf16[1024,128]{0,1:T(8,128)(2,1)}, bf16[1024,128]{0,1:T(8,128)(2,1)S(1)}, u32[]{:S(2)}) copy-start(bf16[1024,128]{0,1:T(8,128)(2,1)S(1)} %collective-permute-done.1) | copy-start | bytes 786436
  188.6 8.6 %collective-permute-start.2 = (bf16[1024,128]{0,1:T(8,128)(2,1)S(1)}, bf16[1024,128]{0,1:T(8,128)(2,1)S(1)}, u32[]{:S(2)}, u32[]{:S(2)}) collective-permute-start(bf16[1024,128]{0,1:T(8,128)(2,1)S(1)} %collective-permute-done.1), channel_id=1, source_target_pairs={{0,1},{1,2},{2,3},{3,4},{4,5},{5,6},{6,7},{7,8},{8,9},{9,10},{10,1... | collective-permute-start | bytes 786440 | tf_op jit(solution)/shard_map/ppermute | solution.py:131
  188.6 0.7 copy-start.3
  189.3 8.4 %collective-permute-start.9 = (bf16[1024,128]{0,1:T(8,128)(2,1)S(1)}, bf16[1024,128]{0,1:T(8,128)(2,1)S(1)}, u32[]{:S(2)}, u32[]{:S(2)}) collective-permute-start(bf16[1024,128]{0,1:T(8,128)(2,1)S(1)} %collective-permute-done.8), channel_id=1, source_target_pairs={{0,15},{1,0},{2,1},{3,2},{4,3},{5,4},{6,5},{7,6},{8,7},{9,8},{10,9... | collective-permute-start | bytes 786440 | tf_op jit(solution)/shard_map/ppermute | solution.py:134
  197.2 9.2 %copy-start.9 = (bf16[1024,128]{0,1:T(8,128)(2,1)}, bf16[1024,128]{0,1:T(8,128)(2,1)S(1)}, u32[]{:S(2)}) copy-start(bf16[1024,128]{0,1:T(8,128)(2,1)S(1)} %collective-permute-done.2) | copy-start | bytes 786436
  197.2 8.6 %collective-permute-start.3 = (bf16[1024,128]{0,1:T(8,128)(2,1)S(1)}, bf16[1024,128]{0,1:T(8,128)(2,1)S(1)}, u32[]{:S(2)}, u32[]{:S(2)}) collective-permute-start(bf16[1024,128]{0,1:T(8,128)(2,1)S(1)} %collective-permute-done.2), channel_id=1, source_target_pairs={{0,1},{1,2},{2,3},{3,4},{4,5},{5,6},{6,7},{7,8},{8,9},{9,10},{10,1... | collective-permute-start | bytes 786440 | tf_op jit(solution)/shard_map/ppermute | solution.py:131
  197.7 4.7 copy-start.7
  197.7 8.6 %collective-permute-start.10 = (bf16[1024,128]{0,1:T(8,128)(2,1)S(1)}, bf16[1024,128]{0,1:T(8,128)(2,1)}, u32[]{:S(2)}, u32[]{:S(2)}) collective-permute-start(bf16[1024,128]{0,1:T(8,128)(2,1)S(1)} %collective-permute-done.9), channel_id=1, source_target_pairs={{0,15},{1,0},{2,1},{3,2},{4,3},{5,4},{6,5},{7,6},{8,7},{9,8},{10,9... | collective-permute-start | bytes 786440 | tf_op jit(solution)/shard_map/ppermute | solution.py:134
  205.8 5.4 copy-start.11
  205.8 8.7 %collective-permute-start.4 = (bf16[1024,128]{0,1:T(8,128)(2,1)S(1)}, bf16[1024,128]{0,1:T(8,128)(2,1)}, u32[]{:S(2)}, u32[]{:S(2)}) collective-permute-start(bf16[1024,128]{0,1:T(8,128)(2,1)S(1)} %collective-permute-done.3), channel_id=1, source_target_pairs={{0,1},{1,2},{2,3},{3,4},{4,5},{5,6},{6,7},{7,8},{8,9},{9,10},{10,1... | collective-permute-start | bytes 786440 | tf_op jit(solution)/shard_map/ppermute | solution.py:131
  206.4 9.0 %collective-permute-start.11 = (bf16[1024,128]{0,1:T(8,128)(2,1)}, bf16[1024,128]{0,1:T(8,128)(2,1)}, u32[]{:S(2)}, u32[]{:S(2)}) collective-permute-start(bf16[1024,128]{0,1:T(8,128)(2,1)} %collective-permute-done.10), channel_id=1, source_target_pairs={{0,15},{1,0},{2,1},{3,2},{4,3},{5,4},{6,5},{7,6},{8,7},{9,8},{10,9... | collective-permute-start | bytes 786440 | tf_op jit(solution)/shard_map/ppermute | solution.py:134
  214.5 8.9 %collective-permute-start.5 = (bf16[1024,128]{0,1:T(8,128)(2,1)}, bf16[1024,128]{0,1:T(8,128)(2,1)}, u32[]{:S(2)}, u32[]{:S(2)}) collective-permute-start(bf16[1024,128]{0,1:T(8,128)(2,1)} %collective-permute-done.4), channel_id=1, source_target_pairs={{0,1},{1,2},{2,3},{3,4},{4,5},{5,6},{6,7},{7,8},{8,9},{9,10},{10,1... | collective-permute-start | bytes 786440 | tf_op jit(solution)/shard_map/ppermute | solution.py:131
  214.5 40.7 %copy-start.12 = (bf16[1024,128]{0,1:T(8,128)(2,1)S(1)}, bf16[1024,128]{0,1:T(8,128)(2,1)}, u32[]{:S(2)}) copy-start(bf16[1024,128]{0,1:T(8,128)(2,1)} %copy-done.11) | copy-start | bytes 786436
  214.5 40.8 %copy-start.10 = (bf16[1024,128]{0,1:T(8,128)(2,1)S(1)}, bf16[1024,128]{0,1:T(8,128)(2,1)}, u32[]{:S(2)}) copy-start(bf16[1024,128]{0,1:T(8,128)(2,1)} %copy-done.9) | copy-start | bytes 786436
  214.5 40.8 %copy-start.6 = (bf16[1024,128]{0,1:T(8,128)(2,1)S(1)}, bf16[1024,128]{0,1:T(8,128)(2,1)}, u32[]{:S(2)}) copy-start(bf16[1024,128]{0,1:T(8,128)(2,1)} %copy-done.5) | copy-start | bytes 786436
  214.5 40.9 %copy-start.4 = (bf16[1024,128]{0,1:T(8,128)(2,1)S(1)}, bf16[1024,128]{0,1:T(8,128)(2,1)}, u32[]{:S(2)}) copy-start(bf16[1024,128]{0,1:T(8,128)(2,1)} %copy-done.3) | copy-start | bytes 786436
  214.5 40.9 %copy-start.8 = (bf16[1024,128]{0,1:T(8,128)(2,1)S(1)}, bf16[1024,128]{0,1:T(8,128)(2,1)}, u32[]{:S(2)}) copy-start(bf16[1024,128]{0,1:T(8,128)(2,1)} %copy-done.7) | copy-start | bytes 786436
  215.4 8.9 %collective-permute-start.12 = (bf16[1024,128]{0,1:T(8,128)(2,1)}, bf16[1024,128]{0,1:T(8,128)(2,1)S(1)}, u32[]{:S(2)}, u32[]{:S(2)}) collective-permute-start(bf16[1024,128]{0,1:T(8,128)(2,1)} %collective-permute-done.11), channel_id=1, source_target_pairs={{0,15},{1,0},{2,1},{3,2},{4,3},{5,4},{6,5},{7,6},{8,7},{9,8},{10,9... | collective-permute-start | bytes 786440 | tf_op jit(solution)/shard_map/ppermute | solution.py:134
  223.4 8.7 %collective-permute-start.6 = (bf16[1024,128]{0,1:T(8,128)(2,1)}, bf16[1024,128]{0,1:T(8,128)(2,1)S(1)}, u32[]{:S(2)}, u32[]{:S(2)}) collective-permute-start(bf16[1024,128]{0,1:T(8,128)(2,1)} %collective-permute-done.5), channel_id=1, source_target_pairs={{0,1},{1,2},{2,3},{3,4},{4,5},{5,6},{6,7},{7,8},{8,9},{9,10},{10,1... | collective-permute-start | bytes 786440 | tf_op jit(solution)/shard_map/ppermute | solution.py:131
  224.3 11.5 %collective-permute-start.13 = (bf16[1024,128]{0,1:T(8,128)(2,1)S(1)}, bf16[1024,128]{0,1:T(8,128)(2,1)S(1)}, u32[]{:S(2)}, u32[]{:S(2)}) collective-permute-start(bf16[1024,128]{0,1:T(8,128)(2,1)S(1)} %collective-permute-done.12), channel_id=1, source_target_pairs={{0,15},{1,0},{2,1},{3,2},{4,3},{5,4},{6,5},{7,6},{8,7},{9,8},{10,9... | collective-permute-start | bytes 786440 | tf_op jit(solution)/shard_map/ppermute | solution.py:134
  232.1 21.1 %collective-permute-start.7 = (bf16[1024,128]{0,1:T(8,128)(2,1)S(1)}, bf16[1024,128]{0,1:T(8,128)(2,1)S(1)}, u32[]{:S(2)}, u32[]{:S(2)}) collective-permute-start(bf16[1024,128]{0,1:T(8,128)(2,1)S(1)} %collective-permute-done.6), channel_id=1, source_target_pairs={{0,1},{1,2},{2,3},{3,4},{4,5},{5,6},{6,7},{7,8},{8,9},{9,10},{10,1... | collective-permute-start | bytes 786440 | tf_op jit(solution)/shard_map/ppermute | solution.py:131
  235.8 21.7 %collective-permute-start.14 = (bf16[1024,128]{0,1:T(8,128)(2,1)S(1)}, bf16[1024,128]{0,1:T(8,128)(2,1)S(1)}, u32[]{:S(2)}, u32[]{:S(2)}) collective-permute-start(bf16[1024,128]{0,1:T(8,128)(2,1)S(1)} %collective-permute-done.13), channel_id=1, source_target_pairs={{0,15},{1,0},{2,1},{3,2},{4,3},{5,4},{6,5},{7,6},{8,7},{9,8},{10,9... | collective-permute-start | bytes 786440 | tf_op jit(solution)/shard_map/ppermute | solution.py:134
  285.1 21.4 %copy-start.19 = (f32[64]{0:T(128)S(1)}, f32[64]{0:T(128)}, u32[]{:S(2)}) copy-start(f32[64]{0:T(128)} %param.9) | copy-start | bytes 772
  361.3 212.0 %all-gather.2.cloned.1.call-start = ((), (), s32[]{:S(2)}) async-start(), calls=%async_computation.4 | async-start | bytes 4456448 | tf_op jit(solution)/shard_map/all_gather | solution.py:190
  485.9 12.4 %copy-start.13 = (f32[1024,1,64]{2,1,0:T(1,128)S(1)}, f32[1024,1,64]{2,1,0:T(1,128)}, u32[]{:S(2)}) copy-start(f32[1024,1,64]{2,1,0:T(1,128)} %fusion.115) | copy-start | bytes 786436
  509.6 12.5 %copy-start.2 = (f32[1024,64]{1,0:T(8,128)S(1)}, f32[1024,64]{1,0:T(8,128)}, u32[]{:S(2)}) copy-start(f32[1024,64]{1,0:T(8,128)} %copy.147) | copy-start | bytes 786436
  588.0 19.6 %copy-start.15 = (bf16[64,1,2,32]{0,3,1,2:T(8,128)(2,1)S(1)}, bf16[64,1,2,32]{0,3,1,2:T(8,128)(2,1)}, u32[]{:S(2)}) copy-start(bf16[64,1,2,32]{0,3,1,2:T(8,128)(2,1)} %copy-done.14) | copy-start | bytes 24580
  588.0 19.6 %copy-start.17 = (bf16[64,1,2,32]{0,3,1,2:T(8,128)(2,1)S(1)}, bf16[64,1,2,32]{0,3,1,2:T(8,128)(2,1)}, u32[]{:S(2)}) copy-start(bf16[64,1,2,32]{0,3,1,2:T(8,128)(2,1)} %copy-done.16) | copy-start | bytes 24580
  588.0 31.4 %copy-start.1 = (bf16[64,2,64,128]{3,2,1,0:T(8,128)(2,1)S(1)}, bf16[64,2,64,128]{3,2,1,0:T(8,128)(2,1)}, u32[]{:S(2)}) copy-start(bf16[64,2,64,128]{3,2,1,0:T(8,128)(2,1)} %param.5) | copy-start | bytes 6291460
Sparse Core Ops, SparseCore 0:
  50.2 107.2 reduce-scatter.2
  361.4 105.4 reduce-scatter.4
  499.3 50.2 all-gather.1
